TPU v7x, 32 devices: a whole 2x2x4 slice. The times are simulated.
32 devices in a mesh: gx: 4 (over z), gy: 4 (over x, core), role: 2 (over y).
Axes of the slice: x: 2, y: 2, z: 4, core: 2. Of those that a mesh axis runs over, the one named last changes fastest.
Arguments:
- velocity: float32 [3, 64, 64, 256], P(None, 'gx', 'gy', 'role'), may hold values from -6 to 6
- target_visc: bfloat16 [32, 32, 128], P('gx', 'gy', 'role'), may hold values from 0.049804688 to 1
- w_first: bfloat16 [64, 81], replicated, may hold values from -2 to 2
- w_hidden: bfloat16 [64, 1728], replicated, may hold values from -0.3125 to 0.3125
- w_last: bfloat16 [64], replicated, may hold values from -1.5 to 1.5
- sample_owner: int32 [4, 2, 32, 1], P('gy', 'role'), may hold values from 0 to 3; in each aligned block of 8 rows (0 to 7, 8 to 15, ..., all dimensions but the last counted through in order) at most 4 rows name the same one
- sample_block: int32 [4, 2, 32, 1], P('gy', 'role'), may hold values from 0 to 7
Outputs:
- u_next: float32 [3, 64, 64, 256], P(None, 'gx', 'gy', 'role')
- slot_loss: float32 [4, 2, 32], P('gy', 'role', 'gx')
- grad_first: float32 [64, 81], replicated
- grad_hidden: float32 [64, 1728], replicated
- grad_last: float32 [64], replicated
Inputs may be any that keep to these rules, and one draw needn't show every extreme that they name: `sample_owner`: within one trainer's 8 rows (aligned blocks of rows) no gx index is named more than 4 times.
All inputs are finite; a program needn't handle non-finite values.
Results may differ from a plain program's by a relative error of at most 0.002.
The roundings to bfloat16 on the way count: a program that leaves them out, or rounds other values in their place, can miss the bound.
Values may be sent and summed in bfloat16 or wider, within the bound.
No kernel may reach another device: no remote copies, remote signals or barrier semaphores. Data moves between devices by JAX's collectives and lax.ppermute only.
A program may use at most 128 MiB of HBM per device.

v0:
```python
import jax
import jax.numpy as jnp
from jax import lax
from jax.experimental import pallas as pl
from jax.experimental.pallas import tpu as pltpu
from jax.sharding import PartitionSpec as P

F32 = jnp.float32
BF16 = jnp.bfloat16
HIGH = lax.Precision.HIGHEST

SIDE = 8
CELLS = SIDE**3
CH = 64
BLK = 8
ROWS = SIDE * SIDE * BLK
WIDE = SIDE * CH
SLAB = SIDE * BLK
HIDDEN_TILES = 14
TILES = 16
LAST_COL = 81
LOSS_COL = 82

EDDY_SCALE = 2.0**-9
F16 = jnp.float16

base_visc = 0.02
time_step = 0.2


def iota(shape, dim):
    return lax.broadcasted_iota(jnp.int32, shape, dim)


def onehot(cond, dtype=BF16):
    return jnp.where(cond, 1.0, 0.0).astype(dtype)


def sigmoid(v):
    return 0.5 + 0.5 * jnp.tanh(0.5 * v)


def nt(a, b, precision=None):
    return lax.dot_general(a, b, (((1,), (1,)), ((), ())), preferred_element_type=F32, precision=precision)


def tn(a, b, precision=None):
    return lax.dot_general(a, b, (((0,), (0,)), ((), ())), preferred_element_type=F32, precision=precision)


def nn(a, b, precision=None):
    return lax.dot_general(a, b, (((1,), (0,)), ((), ())), preferred_element_type=F32, precision=precision)


def core_half(at):
    return (at ^ (at >> 1)) & 1


def place():
    gx_at, gy_at = lax.axis_index("gx"), lax.axis_index("gy")
    return gx_at, gy_at, core_half(gy_at) == 1


def times_sampled(own, blk, gx_at):
    code = own[...] * BLK + blk[...]
    wanted = gx_at * BLK + iota((BLK, code.shape[1]), 0)
    return jnp.sum(jnp.where(code == wanted, 1.0, 0.0), axis=1, keepdims=True)


def tile_places():
    return [(q, w, h, 2 * q + w, 2 * q + h) for q in range(2) for w in range(6) for h in range(2)]


def exact(a, selector):
    high = a.astype(BF16)
    rest = a - high.astype(F32)
    mid = rest.astype(BF16)
    low = (rest - mid.astype(F32)).astype(BF16)
    return nn(high, selector) + (nn(mid, selector) + nn(low, selector))


def y_face(dst, vel, eddy, high):
    for c in range(3):
        for i in range(2):
            lo = jnp.concatenate([vel[c, x, i : i + 1, :] for x in range(16)], axis=0)
            hi = jnp.concatenate([vel[c, x, 14 + i : 15 + i, :] for x in range(16)], axis=0)
            dst[(c * 2 + i) * 16 : (c * 2 + i + 1) * 16, :] = jnp.where(high, hi, lo)
    dst[96:104, :] = jnp.where(high, eddy[pl.ds(7, 8, stride=8), :], eddy[pl.ds(0, 8, stride=8), :]) * EDDY_SCALE


def diagonal():
    return iota((1, WIDE), 1) >> 6 == iota((SIDE, 1), 0)


def windows(ref, q):
    return jnp.concatenate(
        [
            ref[dx * SLAB : dx * SLAB + ROWS, j * 512 + q * 128 : j * 512 + q * 128 + 384]
            for dx in range(3)
            for j in range(3)
        ],
        axis=1,
    )


def shifted_store(dst_ref, x, val):
    zero = jnp.zeros((1, BLK, WIDE), F32)
    lo, hi = (x + 1) * SLAB, (x + 2) * SLAB
    dst_ref[lo:hi, 0:512] = jnp.concatenate([zero, val[:-1]], axis=0).reshape(SLAB, WIDE).astype(BF16)
    dst_ref[lo:hi, 512:1024] = val.reshape(SLAB, WIDE).astype(BF16)
    dst_ref[lo:hi, 1024:1536] = jnp.concatenate([val[1:], zero], axis=0).reshape(SLAB, WIDE).astype(BF16)


def clear_ends(ref):
    ref[0:SLAB, :] = jnp.zeros((SLAB, 1536), BF16)
    ref[9 * SLAB :, :] = jnp.zeros((SLAB, 1536), BF16)


def forward_kernel(
    vel_in, tgt_in, w1_in, w2_in, w3_in, own_in, blk_in,
    keep, send, eddy_out, loss_out, dl_out, ah_s, slope1_s, i1_s, dh_s, tb_s, vel, own, blk,
    pool_s, fp_s, a_s, tt_s, pre_s, slope2_s, dw_s, big_s, gh_s, w2_s,
    tgt, w1, w2, w3, sems,
):
    pairs = ((w2_in, w2), (vel_in, vel), (tgt_in, tgt), (w1_in, w1), (w3_in, w3), (own_in, own), (blk_in, blk))
    copies = [pltpu.make_async_copy(src, dst, sems.at[n]) for n, (src, dst) in enumerate(pairs)]
    for copy in copies:
        copy.start()
    gx_at, gy_at, second = place()
    trainers = lax.axis_size("gx") * lax.axis_size("gy") * lax.axis_size("role")

    fp_s[...] = jnp.zeros(fp_s.shape, F32)
    clear_ends(a_s)
    w2_s[:, 1664:1792] = jnp.zeros((64, 128), F32)
    zero_tile = jnp.zeros((64, 128), BF16)
    for q, w, h, z, m in tile_places():
        for k in range(9):
            at, cols = k * 384 + w * 64, slice(h * 128, (h + 1) * 128)
            if not -1 <= z - 2 * m <= 2:
                tt_s[q, at : at + 64, cols] = zero_tile
                tb_s[q, at : at + 64, cols] = zero_tile
    for copy in copies:
        copy.wait()

    for c in range(3):
        for x in range(SIDE):
            both = vel[c, 2 * x] + vel[c, 2 * x + 1]
            pool_s[c, x] = both
    rows = []
    for c in range(3):
        cols = []
        for x in range(SIDE):
            cols.append(pool_s[c, x, pl.ds(0, 8, stride=2), :] + pool_s[c, x, pl.ds(1, 8, stride=2), :])
        rows.append(jnp.concatenate(cols, axis=0))
    pooled = jnp.concatenate(rows, axis=0)
    zpool = jnp.where(iota((128, 1), 0) >> 1 == iota((1, 64), 1), 0.125, 0.0).astype(BF16)
    filt = exact(pooled, zpool).astype(BF16)
    tgt_rows = tgt[...].reshape(64, 64)
    zsel = jnp.concatenate([filt[0:64], filt[64:128], filt[128:192], tgt_rows], axis=1)
    spread = onehot(iota((ROWS, 1), 0) >> 3 == iota((1, 64), 1))
    by_block = nn(spread, zsel)
    mine = (iota((1, 256), 1) & 63) >> 3 == iota((ROWS, 1), 0) & 7
    by_block = jnp.where(mine, by_block, 0.0).astype(BF16)
    lane_in = iota((1, 256), 1)
    lane_off = lax.div(lane_in, 24)
    lane_cz = lane_in - lane_off * 24
    src = iota((256, 1), 0)
    pick = onehot(jnp.where(lane_in < 216, lane_cz, -1) == (src >> 6) * 8 + (src & 7))
    cells = nn(by_block, pick)
    pick_t = onehot(jnp.where(src >= 192, src & 7, -1) == iota((1, SIDE), 1))
    target = nn(by_block, pick_t)

    fp_s[1:9, 1:9] = cells.reshape(SIDE, SIDE, BLK, 256)
    group = lax.div(iota((1, 1, 1, 256), 3), 24)
    for x in range(SIDE):
        acc = jnp.zeros((1, SIDE, BLK, 256), F32)
        for k in range(9):
            part = fp_s[x + k // 3 : x + k // 3 + 1, k % 3 : k % 3 + SIDE]
            acc = jnp.where(group == k, part, acc)
        i1_s[x * SLAB : (x + 1) * SLAB, :] = acc.reshape(SLAB, 256).astype(BF16)

    j_at = iota((81, 1), 0)
    j_off, j_dz, j_c = lax.div(j_at, 9), lax.rem(lax.div(j_at, 3), 3) - 1, lax.rem(j_at, 3)
    lane_key = jnp.where(lane_in < 216, lane_off * 4 + (lane_cz >> 3), -1)
    same = lane_key == j_off * 4 + j_c
    delta = jnp.where(same, (lane_in & 7) - j_dz, -9)
    w1v = w1[...]
    t1 = jnp.concatenate([nn(w1v, onehot(delta == z)).astype(BF16) for z in range(SIDE)], axis=0)
    pre_s[...] = nt(i1_s[...], t1)

    src = iota((320, 1), 0) - 64
    dst = iota((1, 512), 1)
    wanted = ((dst >> 7) - 2 + ((dst & 127) >> 6)) * 64 + (dst & 63)
    chooser = onehot(jnp.where((src >= 0) & (src < 192), src - 64, -999) == wanted)
    left = iota((64, 128), 1) < 64
    w2_s[:, 0:1728] = w2[...].astype(F32)
    w2t = jnp.concatenate(
        [
            jnp.transpose(jnp.concatenate([w2_s[:, t * 128 : (t + 1) * 128]] * 2, axis=0))
            for t in range(14)
        ],
        axis=0,
    )
    for k in range(9):
        base = (192 * k) // 128 * 128
        off = 192 * k - base
        width = min(256, 1728 - base)
        tiles = nn(w2[:, base : base + width], chooser[64 - off : 64 - off + width]).astype(BF16)
        kb = 8 - k
        turned = {dz: w2t[(3 * k + dz + 1) * 64 : (3 * k + dz + 2) * 64] for dz in (-1, 0, 1)}
        turned[-2] = turned[2] = jnp.zeros((64, 128), F32)
        forward = {d: jnp.where(left, turned[d], turned[d - 1]).astype(BF16) for d in (-1, 0, 1, 2)}
        for q, w, h, z, m in tile_places():
            at, cols = k * 384 + w * 64, slice(h * 128, (h + 1) * 128)
            if z - 2 * m in forward:
                tt_s[q, at : at + 64, cols] = forward[z - 2 * m]
            d = 2 * m - z
            at = kb * 384 + w * 64
            if -2 <= d <= 1:
                tb_s[q, at : at + 64, cols] = tiles[:, (d + 2) * 128 : (d + 3) * 128]

    for x in range(SIDE):
        pre = pre_s[x * SLAB : (x + 1) * SLAB, :]
        sig = sigmoid(pre)
        slope1_s[x * SLAB : (x + 1) * SLAB, :] = sig * (1.0 + pre * (1.0 - sig))
        shifted_store(a_s, x, (pre * sig).reshape(SIDE, BLK, WIDE))

    for q in range(2):
        pre_s[:, q * 256 : (q + 1) * 256] = nn(windows(a_s, q), tt_s[q])
    for x in range(SIDE):
        pre = pre_s[x * SLAB : (x + 1) * SLAB, :]
        sig = sigmoid(pre)
        slope2_s[x * SLAB : (x + 1) * SLAB, :] = sig * (1.0 + pre * (1.0 - sig))
        ah_s[x * SLAB : (x + 1) * SLAB, :] = (pre * sig).astype(BF16)

    tile8 = onehot(iota((64, 1), 0) == iota((1, WIDE), 1) & 63)
    w3_wide = nn(w3[...], tile8)
    diag = diagonal()
    last = jnp.where(diag, w3_wide, 0.0).astype(BF16)
    logits = nt(ah_s[...], last)
    eddy = 0.5 * (jnp.maximum(logits, 0.0) + jnp.log1p(jnp.exp(-jnp.abs(logits))))
    error = eddy - target
    losses = jnp.sum(jnp.sum((error * error).reshape(64, BLK, SIDE), axis=0), axis=1, keepdims=True) / CELLS
    d_logit = (error * sigmoid(logits) / (trainers * CELLS)).astype(BF16)

    zrep = onehot(iota((SIDE, 1), 0) == (iota((1, 128), 1) & 15) >> 1)
    fine = exact(eddy, zrep)
    fine = jnp.where(iota((1, 128), 1) >> 4 == iota((ROWS, 1), 0) & 7, fine, 0.0)
    fine = jnp.sum(fine.reshape(64, BLK, 128), axis=1)
    eddy_out[...] = fine
    y_face(send.at[HIDDEN_TILES * 32 : HIDDEN_TILES * 32 + 104], vel, eddy_out, gy_at & 1 == 0)
    loss_out[...] = jnp.broadcast_to(losses, (BLK, 128))
    dl_out[...] = d_logit.astype(F32)

    count = times_sampled(own, blk, gx_at)
    big_s[:, 0:512] = nn(d_logit, last)
    for x in range(SIDE):
        d_hid = big_s[x * SLAB : (x + 1) * SLAB, 0:512] * slope2_s[x * SLAB : (x + 1) * SLAB, :]
        d_hid = d_hid.astype(BF16)
        dh_s[x * SLAB : (x + 1) * SLAB, :] = d_hid
        d_hid = d_hid.astype(F32).reshape(SIDE, BLK, WIDE)
        dw_s[x * SLAB : (x + 1) * SLAB, :] = (d_hid * count[None]).reshape(SLAB, WIDE).astype(BF16)
    dwt = jnp.transpose(dw_s[...])

    sums = {}
    for p in range(4):
        first, last_z = max(2 * p - 1, 0), min(2 * p + 2, SIDE - 1)
        shifts = [
            a_s[dx * SLAB : dx * SLAB + ROWS, j * 512 + p * 128 : j * 512 + (p + 1) * 128]
            for dx in range(3)
            for j in range(3)
        ]
        found = nn(dwt[first * 64 : (last_z + 1) * 64], jnp.concatenate(shifts, axis=1))
        for z in range(first, last_z + 1):
            part = found[(z - first) * 64 : (z - first + 1) * 64]
            m = z - 2 * p
            sums[m] = part if m not in sums else sums[m] + part
    low_half = iota((64, 128), 1) < 64
    held = None
    for k in range(9):
        for dz in (-1, 0, 1):
            low, high = (sums[m][:, k * 128 : (k + 1) * 128] for m in (-dz, 1 - dz))
            at = (k * 3 + dz + 1) * 64
            if at % 128:
                gh_s[:, at - 64 : at + 64] = jnp.where(low_half, held, high + pltpu.roll(low, 64, 1))
            else:
                held = low + pltpu.roll(high, 64, 1)
    gh_s[:, 1664:1792] = jnp.where(low_half, held, 0.0)

    for t in range(HIDDEN_TILES):
        top, bottom = (gh_s[r : r + 32, t * 128 : (t + 1) * 128] for r in (0, 32))
        keep[t * 32 : (t + 1) * 32, :] = jnp.where(second, bottom, top)
        send[t * 32 : (t + 1) * 32, :] = jnp.where(second, top, bottom)


def backward_kernel(
    vel, own, blk, eddy, losses, dl_in, ah_s, slope1_s, i1_s, dh_s, tb_s,
    extra_out, halo1, halo2, halo3, halo4, hx_a, hx_b, hy_b, hz, d_s, pre_s, dw_s,
):
    gx_at, gy_at, second = place()
    gx_odd, gy_odd = gx_at & 1 == 1, gy_at & 1 == 1
    dev = (gx_at * lax.axis_size("gy") + gy_at) * lax.axis_size("role") + lax.axis_index("role")
    count = times_sampled(own, blk, gx_at)

    clear_ends(d_s)
    for x in range(SIDE):
        d_hid = dh_s[x * SLAB : (x + 1) * SLAB, :].astype(F32)
        shifted_store(d_s, x, d_hid.reshape(SIDE, BLK, WIDE))

    for c in range(3):
        for i in range(2):
            lo, hi = vel[c, i], vel[c, 14 + i]
            at = (c * 2 + i) * 16
            hx_a[at : at + 16, :] = jnp.where(gx_odd, lo, hi)
            hx_b[at : at + 16, :] = jnp.where(gx_odd, hi, lo)
    fine = eddy[...]
    small = fine * EDDY_SCALE
    hx_a[96:104, :] = jnp.where(gx_odd, small[0:8], small[56:64])
    hx_b[96:104, :] = jnp.where(gx_odd, small[56:64], small[0:8])
    y_face(hy_b, vel, eddy, gy_odd)
    vt = jnp.transpose(vel[...].reshape(768, 128))
    et = jnp.transpose(jnp.concatenate([small, jnp.zeros((64, 128), F32)], axis=0))
    hz[...] = jnp.zeros(hz.shape, F32)
    for t in range(6):
        hz[t * 8 : t * 8 + 2, :] = vt[0:2, t * 128 : (t + 1) * 128]
        hz[t * 8 + 2 : t * 8 + 4, :] = vt[126:128, t * 128 : (t + 1) * 128]
    hz[48:49, :] = et[0:1]
    hz[49:50, :] = et[127:128]
    halo1[...] = jnp.where(second, hx_a[...], hy_b[...])
    halo2[...] = jnp.where(second, hy_b[...], hx_a[...])
    halo3[...] = jnp.where(second, hx_b[...], hz[...])
    halo4[...] = jnp.where(second, hz[...], hx_b[...])

    for q in range(2):
        pre_s[:, q * 256 : (q + 1) * 256] = nn(windows(d_s, q), tb_s[q])
    for x in range(SIDE):
        rows = slice(x * SLAB, (x + 1) * SLAB)
        d_first = (pre_s[rows, :] * slope1_s[rows, :]).astype(BF16).astype(F32)
        dw_s[rows, :] = (d_first.reshape(SIDE, BLK, WIDE) * count[None]).reshape(SLAB, WIDE).astype(BF16)
    g1 = nn(jnp.transpose(dw_s[...]), i1_s[...])
    z_in = iota((1, 256), 1) & 7
    parts = []
    for dz in (-1, 0, 1):
        tot = jnp.zeros((64, 256), F32)
        for z in range(SIDE):
            if 0 <= z + dz < SIDE:
                tot = tot + jnp.where(z_in == z + dz, g1[z * 64 : (z + 1) * 64], 0.0)
        parts.append(tot)
    r_at = iota((768, 1), 0)
    c_at = iota((1, 128), 1)
    r_lane = r_at & 255
    r_off = lax.div(r_lane, 24)
    r_col = (r_off * 3 + (r_at >> 8)) * 3 + ((r_lane - r_off * 24) >> 3)
    fold = onehot(jnp.where(r_lane < 216, r_col, -1) == c_at)
    g_first = exact(jnp.concatenate(parts, axis=1), fold)

    count_rows = jnp.broadcast_to(count.reshape(1, BLK, 1), (64, BLK, 1)).reshape(ROWS, 1)
    dlw = dl_in[...] * count_rows
    dl_hi = dlw.astype(BF16)
    dl_lo = (dlw - dl_hi.astype(F32)).astype(BF16)
    ah = ah_s[...]
    gl = tn(dl_hi, ah) + tn(dl_lo, ah)
    gl = jnp.where(diagonal(), gl, 0.0)
    fold_o = onehot(iota((1, WIDE), 1) & 63 == iota((64, 1), 0), F32)
    g_last = jnp.sum(nt(fold_o, gl, HIGH), axis=1, keepdims=True)

    lane8 = iota((BLK, 128), 1)
    loss_row = jnp.where(lane8 - (LOSS_COL + BLK * (dev >> 6)) == iota((BLK, 128), 0), losses[...], 0.0)
    loss_row = jnp.sum(loss_row, axis=0, keepdims=True)
    lane = iota((64, 128), 1)
    extra = jnp.where(lane == LAST_COL, g_last, g_first)
    extra = extra + jnp.where(iota((64, 128), 0) == dev & 63, loss_row, 0.0)

    extra_out[...] = extra


def vmem_spec():
    return pl.BlockSpec(memory_space=pltpu.VMEM)


def run_forward(*given):
    velocity, target, w1, w2, w3, own, blk = (pltpu.with_memory_space_constraint(a, pltpu.HBM) for a in given)
    half = pltpu.VMEM((HIDDEN_TILES * 32, 128), F32)
    return pl.pallas_call(
        forward_kernel,
        out_shape=(
            half,
            pltpu.VMEM((HIDDEN_TILES * 32 + 104, 128), F32),
            pltpu.VMEM((64, 128), F32),
            pltpu.VMEM((BLK, 128), F32),
            pltpu.VMEM((ROWS, SIDE), F32),
            pltpu.VMEM((ROWS, WIDE), BF16),
            pltpu.VMEM((ROWS, WIDE), F32),
            pltpu.VMEM((ROWS, 256), BF16),
            pltpu.VMEM((ROWS, WIDE), BF16),
            pltpu.VMEM((2, 3456, 256), BF16),
        )
        + tuple(pltpu.VMEM(a.shape, a.dtype) for a in (velocity, own, blk)),
        in_specs=[pl.BlockSpec(memory_space=pltpu.HBM)] * 7,
        out_specs=tuple(vmem_spec() for _ in range(13)),
        scratch_shapes=[
            pltpu.VMEM((3, SIDE, 16, 128), F32),
            pltpu.VMEM((10, 10, BLK, 256), F32),
            pltpu.VMEM((ROWS + 2 * SLAB, 1536), BF16),
            pltpu.VMEM((2, 3456, 256), BF16),
            pltpu.VMEM((ROWS, WIDE), F32),
            pltpu.VMEM((ROWS, WIDE), F32),
            pltpu.VMEM((ROWS, WIDE), BF16),
            pltpu.VMEM((ROWS, WIDE), F32),
            pltpu.VMEM((64, HIDDEN_TILES * 128), F32),
            pltpu.VMEM((64, 1792), F32),
        ]
        + [pltpu.VMEM(a.shape, a.dtype) for a in (target, w1, w2, w3)]
        + [pltpu.SemaphoreType.DMA((7,))],
        compiler_params=pltpu.CompilerParams(vmem_limit_bytes=40 * 1024 * 1024),
        name="forward",
    )(velocity, target, w1, w2, w3, own, blk)


def run_backward(velocity, own, blk, *kept):
    face = pltpu.VMEM((104, 128), F32)
    return pl.pallas_call(
        backward_kernel,
        out_shape=(pltpu.VMEM((64, 128), F32),) + (face,) * 4,
        in_specs=[vmem_spec()] * 11,
        out_specs=tuple(vmem_spec() for _ in range(5)),
        scratch_shapes=[face] * 4
        + [
            pltpu.VMEM((ROWS + 2 * SLAB, 1536), BF16),
            pltpu.VMEM((ROWS, WIDE), F32),
            pltpu.VMEM((ROWS, WIDE), BF16),
        ],
        compiler_params=pltpu.CompilerParams(vmem_limit_bytes=40 * 1024 * 1024),
        name="backward",
    )(velocity, own, blk, *kept)


def flow_kernel(
    vel, eddy, got0, got1, got2, got3, got4, out, rx_a, rx_b, ry_a, ry_b, rz, vx_s, vy_s, visc_s, ez_s
):
    gx_at, gy_at = lax.axis_index("gx"), lax.axis_index("gy")
    gx_odd, gy_odd = gx_at & 1 == 1, gy_at & 1 == 1
    second = core_half(gy_at) == 1
    ry_a[...] = got0[...]
    ry_b[...] = jnp.where(second, got2[...], got1[...])
    rx_a[...] = jnp.where(second, got1[...], got2[...])
    rx_b[...] = jnp.where(second, got3[...], got4[...])
    rz[...] = jnp.where(second, got4[...], got3[...])
    lane = iota((1, 128), 1)

    def sides(odd, a, b, at, rows):
        one, two = a[at : at + rows, :], b[at : at + rows, :]
        return jnp.where(odd, one, two), jnp.where(odd, two, one)

    for c in range(3):
        for x in range(16):
            vy_s[(c * 16 + x) * 32 + 8 : (c * 16 + x) * 32 + 24, :] = vel[c, x]
        for i in range(2):
            below, above = sides(gy_odd, ry_a, ry_b, (c * 2 + i) * 16, 16)
            vy_s[pl.ds(c * 512 + 6 + i, 16, stride=32), :] = below
            vy_s[pl.ds(c * 512 + 24 + i, 16, stride=32), :] = above
            below, above = sides(gx_odd, rx_a, rx_b, (c * 2 + i) * 16, 16)
            vx_s[c, i] = below
            vx_s[c, 2 + i] = above

    zcols = jnp.concatenate([jnp.transpose(rz[t * 8 : t * 8 + 8, :]) for t in range(7)], axis=0)
    coarse = eddy[...]
    e_first, e_last = zcols[768:832, 0:1] / EDDY_SCALE, zcols[768:832, 1:2] / EDDY_SCALE
    ahead = jnp.where(lane == 127, e_first, pltpu.roll(coarse, 127, 1))
    behind = jnp.where(lane == 0, e_last, pltpu.roll(coarse, 1, 1))
    below_x, above_x = (v / EDDY_SCALE for v in sides(gx_odd, rx_a, rx_b, 96, 8))
    below_y, above_y = (v / EDDY_SCALE for v in sides(gy_odd, ry_a, ry_b, 96, 8))

    def put(dst, plane, val):
        dst[pl.ds(plane * 32 + 8, 8, stride=2), :] = val
        dst[pl.ds(plane * 32 + 9, 8, stride=2), :] = val

    put(visc_s, 0, base_visc + below_x)
    put(visc_s, 17, base_visc + above_x)
    for x in range(8):
        for r in range(2):
            plane = 2 * x + 1 + r
            put(visc_s, plane, base_visc + coarse[x * 8 : x * 8 + 8])
            visc_s[plane * 32 + 7 : plane * 32 + 8, :] = base_visc + below_y[x : x + 1]
            visc_s[plane * 32 + 24 : plane * 32 + 25, :] = base_visc + above_y[x : x + 1]
        put(ez_s, 2 * x, base_visc + ahead[x * 8 : x * 8 + 8])
        put(ez_s, 2 * x + 1, base_visc + behind[x * 8 : x * 8 + 8])

    def plane_of(c, x):
        if x < 0:
            return vx_s[c, x + 2]
        if x > 15:
            return vx_s[c, x - 14]
        return vel[c, x]

    for x in range(16):
        vat = (x + 1) * 32
        visc = visc_s[vat + 8 : vat + 24, :]
        faces = (
            (visc_s[vat + 40 : vat + 56, :], visc_s[vat - 24 : vat - 8, :]),
            (visc_s[vat + 9 : vat + 25, :], visc_s[vat + 7 : vat + 23, :]),
            (
                ez_s[(x // 2 * 2) * 32 + 8 : (x // 2 * 2) * 32 + 24, :],
                ez_s[(x // 2 * 2 + 1) * 32 + 8 : (x // 2 * 2 + 1) * 32 + 24, :],
            ),
        )
        faces = [(0.5 * (visc + a), 0.5 * (visc + b)) for a, b in faces]
        wind = [vel[a, x] for a in range(3)]
        for c in range(3):
            u = vel[c, x]
            at = (c * 16 + x) * 32
            zat = (c * 16 + x) * 16
            zc = zcols[zat : zat + 16]
            p1 = jnp.where(lane == 127, zc[:, 0:1], pltpu.roll(u, 127, 1))
            p2 = jnp.where(lane == 127, zc[:, 1:2], jnp.where(lane == 126, zc[:, 0:1], pltpu.roll(u, 126, 1)))
            m1 = jnp.where(lane == 0, zc[:, 3:4], pltpu.roll(u, 1, 1))
            m2 = jnp.where(lane == 0, zc[:, 2:3], jnp.where(lane == 1, zc[:, 3:4], pltpu.roll(u, 2, 1)))
            near = (
                (plane_of(c, x + 1), plane_of(c, x - 1), plane_of(c, x + 2), plane_of(c, x - 2)),
                (
                    vy_s[at + 9 : at + 25, :], vy_s[at + 7 : at + 23, :],
                    vy_s[at + 10 : at + 26, :], vy_s[at + 6 : at + 22, :],
                ),
                (p1, m1, p2, m2),
            )
            advect = None
            diffuse = None
            for a in range(3):
                q1, b1, q2, b2 = near[a]
                slope = (8.0 * (q1 - b1) - (q2 - b2)) * (1.0 / 12.0)
                term = wind[a] * slope
                advect = term if advect is None else advect + term
                flux = faces[a][0] * (q1 - u) - faces[a][1] * (u - b1)
                diffuse = flux if diffuse is None else diffuse + flux
            out[c, x] = u + time_step * (diffuse - advect)


def run_flow(velocity, eddy, *got):
    return pl.pallas_call(
        flow_kernel,
        out_shape=jax.ShapeDtypeStruct(velocity.shape, F32),
        in_specs=[vmem_spec()] * 7,
        out_specs=vmem_spec(),
        scratch_shapes=[
            pltpu.VMEM((104, 128), F32),
            pltpu.VMEM((104, 128), F32),
            pltpu.VMEM((104, 128), F32),
            pltpu.VMEM((104, 128), F32),
            pltpu.VMEM((104, 128), F32),
            pltpu.VMEM((3, 4, 16, 128), F32),
            pltpu.VMEM((3 * 16 * 32, 128), F32),
            pltpu.VMEM((18 * 32, 128), F32),
            pltpu.VMEM((16 * 32, 128), F32),
        ],
        compiler_params=pltpu.CompilerParams(vmem_limit_bytes=32 * 1024 * 1024),
        name="flow",
    )(velocity, eddy, *got)


def finish_kernel(own, blk, mine, other, loss_out, first_out, hidden_out, last_out):
    gx_at, gy_at = lax.axis_index("gx"), lax.axis_index("gy")
    n_z = lax.axis_size("role")
    in_group = gy_at * n_z + lax.axis_index("role")
    second = core_half(gy_at) == 1
    for t in range(HIDDEN_TILES):
        one, two = mine[t * 32 : (t + 1) * 32, :], other[t * 32 : (t + 1) * 32, :]
        top, bottom = jnp.where(second, two, one), jnp.where(second, one, two)
        width = min(128, 27 * CH - t * 128)
        hidden_out[0:32, t * 128 : t * 128 + width] = top[:, :width]
        hidden_out[32:64, t * 128 : t * 128 + width] = bottom[:, :width]
    extra = mine[HIDDEN_TILES * 32 :, :] + other[HIDDEN_TILES * 32 :, :]
    first_out[...] = extra[:, 0:81]
    turned = jnp.transpose(jnp.concatenate([extra, jnp.zeros((64, 128), F32)], axis=0))
    last_out[...] = turned[LAST_COL : LAST_COL + 1, 0:64]
    slots = loss_out.shape[1]
    dev = own[...] * (lax.axis_size("gy") * n_z) + in_group
    listed = dev.shape[1]
    pick = onehot(iota((64, listed), 0) == dev & 63, F32)
    rows = nn(turned[:, 0:64], pick, HIGH)
    rows = jnp.where(iota((128, listed), 0) == LOSS_COL + BLK * (dev >> 6) + blk[...], rows, 0.0)
    found = jnp.sum(rows, axis=0, keepdims=True)
    picked = jnp.zeros((1, slots), F32)
    for g in range(listed // slots):
        picked = jnp.where(gx_at == g, found[:, g * slots : (g + 1) * slots], picked)
    loss_out[...] = picked


def run_finish(own, blk, mine, other, slots):
    f = lambda *s: jax.ShapeDtypeStruct(s, F32)
    return pl.pallas_call(
        finish_kernel,
        out_shape=(f(1, slots), f(64, 81), f(64, 27 * CH), f(1, 64)),
        in_specs=[vmem_spec()] * 4,
        out_specs=tuple(vmem_spec() for _ in range(4)),
        compiler_params=pltpu.CompilerParams(vmem_limit_bytes=32 * 1024 * 1024),
        name="finish",
    )(own, blk, mine, other)


def on_device(velocity, target_visc, w_first, w_hidden, w_last, sample_owner, sample_block):
    n_x, n_y, n_z = lax.axis_size("gx"), lax.axis_size("gy"), lax.axis_size("role")
    trainers = n_x * n_y * n_z
    own = sample_owner.reshape(1, -1)
    blk = sample_block.reshape(1, -1)
    slots = own.shape[1] // n_x

    axes = ("gx", "gy", "role")

    def even_odd(i, count):
        return i ^ 1

    def odd_even(i, count):
        return (i - 1) % count if i % 2 == 0 else (i + 1) % count

    def partner(kind, i, j, r):
        if kind == "x":
            j = odd_even(j, n_y)
        elif kind == "y":
            r = r ^ 1
        elif kind == "z_a":
            i = even_odd(i, n_x)
        else:
            i = odd_even(i, n_x)
        return (i * n_y + j) * n_z + r

    def mixed(kinds):
        pairs = []
        for i in range(n_x):
            for j in range(n_y):
                for r in range(n_z):
                    pairs.append(((i * n_y + j) * n_z + r, partner(kinds[(j ^ (j >> 1)) & 1], i, j, r)))
        return pairs

    core_pairs = [(j, even_odd(j, n_y)) for j in range(n_y)]
    size = TILES * 32

    keep, send, eddy, *kept, velocity, own, blk = run_forward(
        velocity, target_visc, w_first, w_hidden, w_last.reshape(1, CH), own, blk
    )
    half = core_half(lax.axis_index("gy"))
    got = lax.ppermute(send, "gy", core_pairs)
    extra, *halos = run_backward(velocity, own, blk, eddy, *kept)
    total = jnp.concatenate([keep + got[: HIDDEN_TILES * 32], extra], axis=0)
    rims = [got[HIDDEN_TILES * 32 :]]
    halos = [h.astype(F16) for h in halos]

    def widen(values, exps):
        wide = values.astype(F32).reshape(TILES, 32, 128) * jnp.exp2(exps)[:, None, :]
        return wide.reshape(size, 128)

    top = jnp.max(jnp.abs(total.reshape(TILES, 32, 128)), axis=1)
    exps = jnp.clip(jnp.ceil(jnp.log2(jnp.maximum(top, 1e-30))) - 13.0, -110.0, 110.0)
    orders = (("x", "z_a", "y", "z_b"), ("z_a", "x", "z_b", "y"))
    for s in range(4):
        kinds = (orders[0][s], orders[1][s])
        scaled = total.reshape(TILES, 32, 128) * jnp.exp2(-exps)[:, None, :]
        pieces = [scaled.reshape(size, 128).astype(F16), exps.astype(F16)]
        message = jnp.concatenate(pieces + [halos[s]] if s < 3 else pieces, axis=0)
        message = lax.optimization_barrier(message)
        got = lax.ppermute(message, axes, mixed(kinds))
        if s == 1:
            far = lax.ppermute(halos[3], axes, mixed((orders[0][3], orders[1][3])))
        their_exps = got[size : size + TILES].astype(F32)
        mine, theirs = widen(message[:size], exps), widen(got[:size], their_exps)
        if n_x != 4 and "z_b" in kinds:
            theirs = jnp.where(half == kinds.index("z_b"), 0.0, theirs)
        total = mine + theirs
        exps = jnp.maximum(exps, their_exps) + 1.0
        if s < 3:
            rims.append(got[size + 16 :].astype(F32))
        if s == 1:
            total, far = lax.optimization_barrier((total, far))
        if s == 2:
            u_next = run_flow(velocity, eddy, *rims, far.astype(F32))
    total, u_next = lax.optimization_barrier((total, u_next))
    if n_x != 4:
        for bit in range(1, n_x.bit_length() - 1):
            total = total + lax.ppermute(total, "gx", [(i, i ^ (1 << bit)) for i in range(n_x)])
    other = lax.ppermute(total, "gy", core_pairs)

    losses, first, hidden, last = run_finish(own, blk, total, other, slots)
    return (u_next, losses.reshape(1, 1, slots), first, hidden, last.reshape(CH))


def solution(mesh):
    return jax.shard_map(
        on_device,
        mesh=mesh,
        in_specs=(
            P(None, "gx", "gy", "role"),
            P("gx", "gy", "role"),
            P(),
            P(),
            P(),
            P("gy", "role", None, None),
            P("gy", "role", None, None),
        ),
        out_specs=(P(None, "gx", "gy", "role"), P("gy", "role", "gx"), P(), P(), P()),
        check_vma=False,
    )
```

profile of v0, /device:TPU:0, one launch (start us, length us, event | category | flops | bytes accessed | tf_op | source)
XLA Modules:
  0.0 39.7 jit_solution(1899841618960902724)
XLA Ops:
  0.6 7.3 %forward.1 = (f32[448,128]{1,0:T(8,128)S(1)}, f32[552,128]{1,0:T(8,128)S(1)}, f32[64,128]{1,0:T(8,128)S(1)}, f32[8,128]{1,0:T(8,128)S(1)}, f32[512,8]{1,0:T(8,12...) custom-call(f32[3,16,16,128]{3,2,1,0:T(8,128)} %vel_in.1, ...), custom_call_target="tpu_custom_call" | custom-call | tf_op jit(solution)/shard_map/forward/pallas_call | solution.py:384
  7.9 0.5 %collective-permute-start = (f32[552,128]{1,0:T(8,128)S(1)}, f32[552,128]{1,0:T(8,128)S(1)}, u32[]{:S(2)}, u32[]{:S(2)}) collective-permute-start(f32[552,128]{1,0:T(8,128)S(1)} %get-tuple-element.32), channel_id=1, source_target_pairs={{0,2},{2,0},{4,6},{6,4},{1,3},{3,1},{5,7},{7,5},{8,10},{10,8},{12,... | collective-permute-start | bytes 847880 | tf_op jit(solution)/shard_map/ppermute | solution.py:641
  8.5 3.4 %backward.1 = (f32[64,128]{1,0:T(8,128)S(1)}, f32[104,128]{1,0:T(8,128)S(1)}, f32[104,128]{1,0:T(8,128)S(1)}, f32[104,128]{1,0:T(8,128)S(1)}, f32[104,128]{1,0:T(8,128)S(1)}) custom-call(f32[3,16,16,128]{3,2,1,0:T(8,128)S(1)} %get-tuple-element.33.vel, s32[1,32]{1,0:T(1,128)S(1)} %get-tuple-element.34.own, s32[1,32]{1,0:T(1,128)S(1)} %get-tuple-element.35.blk, ...), custom_call_target="tpu_custom_call" | custom-call | tf_op jit(solution)/shard_map/backward/pallas_call | solution.py:422
  12.1 0.1 pad_maximum_fusion.1
  12.1 2.7 %collective-permute-start.1 = (f16[632,128]{1,0:T(8,128)(2,1)S(1)}, f16[632,128]{1,0:T(8,128)(2,1)S(1)}, u32[]{:S(2)}, u32[]{:S(2)}) collective-permute-start(f16[632,128]{1,0:T(8,128)(2,1)S(1)} %pad_maximum_fusion.1), channel_id=1, source_target_pairs={{0,6},{1,7},{2,10},{3,11},{4,12},{5,13},{6,0},{7,1},{8,14},{9,15},... | collective-permute-start | bytes 485384 | tf_op jit(solution)/shard_map/ppermute | solution.py:660
  14.8 3.7 %collective-permute-start.3 = (f16[104,128]{1,0:T(8,128)(2,1)S(1)}, f16[104,128]{1,0:T(8,128)(2,1)S(1)}, u32[]{:S(2)}, u32[]{:S(2)}) collective-permute-start(f16[104,128]{1,0:T(8,128)(2,1)S(1)} %convert_element_type.96), channel_id=1, source_target_pairs={{0,24},{1,25},{2,3},{3,2},{4,5},{5,4},{6,30},{7,31},{8,16},{9,17},... | collective-permute-start | bytes 79880 | tf_op jit(solution)/shard_map/ppermute | solution.py:662
  18.5 0.0 collective-permute-done.1
  18.6 0.1 fusion.5
  18.6 0.1 pad_maximum_fusion.2
  18.7 1.1 %collective-permute-start.2 = (f16[632,128]{1,0:T(8,128)(2,1)S(1)}, f16[632,128]{1,0:T(8,128)(2,1)S(1)}, u32[]{:S(2)}, u32[]{:S(2)}) collective-permute-start(f16[632,128]{1,0:T(8,128)(2,1)S(1)} %pad_maximum_fusion.2), channel_id=1, source_target_pairs={{0,8},{1,9},{2,4},{3,5},{4,2},{5,3},{6,14},{7,15},{8,0},{9,1},{10,... | collective-permute-start | bytes 485384 | tf_op jit(solution)/shard_map/ppermute | solution.py:660
  19.8 4.3 %collective-permute-done.2 = f16[632,128]{1,0:T(8,128)(2,1)S(1)} collective-permute-done((f16[632,128]{1,0:T(8,128)(2,1)S(1)}, f16[632,128]{1,0:T(8,128)(2,1)S(1)}, u32[]{:S(2)}, u32[]{:S(2)}) %collective-permute-start.2) | collective-permute-done | bytes 161824 | tf_op jit(solution)/shard_map/ppermute | solution.py:660
  24.1 0.1 fusion.4
  24.2 0.0 collective-permute-done.3
  24.2 0.1 pad_maximum_fusion.3
  24.3 1.6 %collective-permute-start.4 = (f16[632,128]{1,0:T(8,128)(2,1)S(1)}, f16[632,128]{1,0:T(8,128)(2,1)S(1)}, u32[]{:S(2)}, u32[]{:S(2)}) collective-permute-start(f16[632,128]{1,0:T(8,128)(2,1)S(1)} %pad_maximum_fusion.3), channel_id=1, source_target_pairs={{0,1},{1,0},{2,26},{3,27},{4,28},{5,29},{6,7},{7,6},{8,9},{9,8},{1... | collective-permute-start | bytes 485384 | tf_op jit(solution)/shard_map/ppermute | solution.py:660
  25.9 3.8 %collective-permute-done.4 = f16[632,128]{1,0:T(8,128)(2,1)S(1)} collective-permute-done((f16[632,128]{1,0:T(8,128)(2,1)S(1)}, f16[632,128]{1,0:T(8,128)(2,1)S(1)}, u32[]{:S(2)}, u32[]{:S(2)}) %collective-permute-start.4) | collective-permute-done | bytes 161824 | tf_op jit(solution)/shard_map/ppermute | solution.py:660
  29.7 0.1 fusion.1
  29.8 3.1 %collective-permute-start.5 = (f16[528,128]{1,0:T(8,128)(2,1)S(1)}, f16[528,128]{1,0:T(8,128)(2,1)S(1)}, u32[]{:S(2)}, u32[]{:S(2)}) collective-permute-start(f16[528,128]{1,0:T(8,128)(2,1)S(1)} %pad_maximum_fusion.4), channel_id=1, source_target_pairs={{0,24},{1,25},{2,3},{3,2},{4,5},{5,4},{6,30},{7,31},{8,16},{9,17},... | collective-permute-start | bytes 405512 | tf_op jit(solution)/shard_map/ppermute | solution.py:660
  32.9 2.6 %flow.1 = f32[3,16,16,128]{3,2,1,0:T(8,128)} custom-call(f32[3,16,16,128]{3,2,1,0:T(8,128)S(1)} %get-tuple-element.33.vel, f32[64,128]{1,0:T(8,128)S(1)} %get-tuple-element.36.eddy, f32[104,128]{1,0:T(8,128)S(1)} %slice.81.got0, f32[104,128]{1,0:T(8,128)S(1)} %slice_convert_fusion.2.got1, f32[104,128]{1,0:T(8,128)S(1)} %slice_convert_fusion.1.got2, ...), custom_call_target="tpu_custom_call" | custom-call | tf_op jit(solution)/shard_map/flow/pallas_call | solution.py:539
  35.5 1.2 %collective-permute-done.5 = f16[528,128]{1,0:T(8,128)(2,1)S(1)} collective-permute-done((f16[528,128]{1,0:T(8,128)(2,1)S(1)}, f16[528,128]{1,0:T(8,128)(2,1)S(1)}, u32[]{:S(2)}, u32[]{:S(2)}) %collective-permute-start.5) | collective-permute-done | bytes 135200 | tf_op jit(solution)/shard_map/ppermute | solution.py:660
  36.8 0.1 fusion.mine
  36.8 0.1 collective-permute-start.6
  36.9 1.5 %collective-permute-done.6.other = f32[512,128]{1,0:T(8,128)S(1)} collective-permute-done((f32[512,128]{1,0:T(8,128)S(1)}, f32[512,128]{1,0:T(8,128)S(1)}, u32[]{:S(2)}, u32[]{:S(2)}) %collective-permute-start.6) | collective-permute-done | bytes 262176 | tf_op jit(solution)/shard_map/ppermute | solution.py:679
  38.4 1.3 %finish.1 = (f32[1,8]{1,0:T(1,128)}, f32[64,81]{1,0:T(8,128)}, f32[64,1728]{1,0:T(8,128)}, f32[1,64]{1,0:T(1,128)}) custom-call(s32[1,32]{1,0:T(1,128)S(1)} %get-tuple-element.34.own, s32[1,32]{1,0:T(1,128)S(1)} %get-tuple-element.35.blk, f32[512,128]{1,0:T(8,128)S(1)} %fusion.mine, f32[512,128]{1,0:T(8,128)S(1)} %collective-permute-done.6.other), custom_call_target="tpu_custom_call" | custom-call | tf_op jit(solution)/shard_map/finish/pallas_call | solution.py:590
  (21 shorter events, 0.3 us)
Async XLA Ops:
  7.9 4.0 %collective-permute-start = (f32[552,128]{1,0:T(8,128)S(1)}, f32[552,128]{1,0:T(8,128)S(1)}, u32[]{:S(2)}, u32[]{:S(2)}) collective-permute-start(f32[552,128]{1,0:T(8,128)S(1)} %get-tuple-element.32), channel_id=1, source_target_pairs={{0,2},{2,0},{4,6},{6,4},{1,3},{3,1},{5,7},{7,5},{8,10},{10,8},{12,... | collective-permute-start | bytes 847880 | tf_op jit(solution)/shard_map/ppermute | solution.py:641
  12.1 6.4 %collective-permute-start.1 = (f16[632,128]{1,0:T(8,128)(2,1)S(1)}, f16[632,128]{1,0:T(8,128)(2,1)S(1)}, u32[]{:S(2)}, u32[]{:S(2)}) collective-permute-start(f16[632,128]{1,0:T(8,128)(2,1)S(1)} %pad_maximum_fusion.1), channel_id=1, source_target_pairs={{0,6},{1,7},{2,10},{3,11},{4,12},{5,13},{6,0},{7,1},{8,14},{9,15},... | collective-permute-start | bytes 485384 | tf_op jit(solution)/shard_map/ppermute | solution.py:660
  14.8 9.3 %collective-permute-start.3 = (f16[104,128]{1,0:T(8,128)(2,1)S(1)}, f16[104,128]{1,0:T(8,128)(2,1)S(1)}, u32[]{:S(2)}, u32[]{:S(2)}) collective-permute-start(f16[104,128]{1,0:T(8,128)(2,1)S(1)} %convert_element_type.96), channel_id=1, source_target_pairs={{0,24},{1,25},{2,3},{3,2},{4,5},{5,4},{6,30},{7,31},{8,16},{9,17},... | collective-permute-start | bytes 79880 | tf_op jit(solution)/shard_map/ppermute | solution.py:662
  18.7 5.4 %collective-permute-start.2 = (f16[632,128]{1,0:T(8,128)(2,1)S(1)}, f16[632,128]{1,0:T(8,128)(2,1)S(1)}, u32[]{:S(2)}, u32[]{:S(2)}) collective-permute-start(f16[632,128]{1,0:T(8,128)(2,1)S(1)} %pad_maximum_fusion.2), channel_id=1, source_target_pairs={{0,8},{1,9},{2,4},{3,5},{4,2},{5,3},{6,14},{7,15},{8,0},{9,1},{10,... | collective-permute-start | bytes 485384 | tf_op jit(solution)/shard_map/ppermute | solution.py:660
  24.3 5.4 %collective-permute-start.4 = (f16[632,128]{1,0:T(8,128)(2,1)S(1)}, f16[632,128]{1,0:T(8,128)(2,1)S(1)}, u32[]{:S(2)}, u32[]{:S(2)}) collective-permute-start(f16[632,128]{1,0:T(8,128)(2,1)S(1)} %pad_maximum_fusion.3), channel_id=1, source_target_pairs={{0,1},{1,0},{2,26},{3,27},{4,28},{5,29},{6,7},{7,6},{8,9},{9,8},{1... | collective-permute-start | bytes 485384 | tf_op jit(solution)/shard_map/ppermute | solution.py:660
  29.8 7.0 %collective-permute-start.5 = (f16[528,128]{1,0:T(8,128)(2,1)S(1)}, f16[528,128]{1,0:T(8,128)(2,1)S(1)}, u32[]{:S(2)}, u32[]{:S(2)}) collective-permute-start(f16[528,128]{1,0:T(8,128)(2,1)S(1)} %pad_maximum_fusion.4), channel_id=1, source_target_pairs={{0,24},{1,25},{2,3},{3,2},{4,5},{5,4},{6,30},{7,31},{8,16},{9,17},... | collective-permute-start | bytes 405512 | tf_op jit(solution)/shard_map/ppermute | solution.py:660
  36.8 1.6 %collective-permute-start.6 = (f32[512,128]{1,0:T(8,128)S(1)}, f32[512,128]{1,0:T(8,128)S(1)}, u32[]{:S(2)}, u32[]{:S(2)}) collective-permute-start(f32[512,128]{1,0:T(8,128)S(1)} %fusion.mine), channel_id=1, source_target_pairs={{0,2},{2,0},{4,6},{6,4},{1,3},{3,1},{5,7},{7,5},{8,10},{10,8},{12,... | collective-permute-start | bytes 786440 | tf_op jit(solution)/shard_map/ppermute | solution.py:679
where the time goes:
time: 39.8 us; the launch traced here: 39.7 us
  Pallas kernels  14.6 us (37%)
  starting transfers between devices  12.6 us (32%)
  waiting for transfers between devices  10.8 us (27%)
  between operations  0.82 us (2%)
  other arithmetic  0.76 us (2%)
    ppermute x4, waiting for transfers between devices, on_device(): got = lax.ppermute(message, axes, mixed(kinds))  9.31 us
    ppermute x4, starting transfers between devices, on_device(): got = lax.ppermute(message, axes, mixed(kinds))  8.4 us
    pallas_call x1, Pallas kernels, run_forward(): pl.pallas_call(forward_kernel, out_shape=(half, pltpu.VMEM((HIDDEN_TILES...  7.31 us
    ppermute x1, starting transfers between devices, on_device(): far = lax.ppermute(halos[3], axes, mixed((orders[0][3], orders[1][3])))  3.67 us
    pallas_call x1, Pallas kernels, run_backward(): pl.pallas_call(backward_kernel, out_shape=(pltpu.VMEM((64, 128), F32),) +...  3.42 us
    pallas_call x1, Pallas kernels, run_flow(): pl.pallas_call(flow_kernel, out_shape=jax.ShapeDtypeStruct(velocity.shape...  2.62 us
    ppermute x1, waiting for transfers between devices, on_device(): other = lax.ppermute(total, 'gy', core_pairs)  1.52 us
    pallas_call x1, Pallas kernels, run_finish(): pl.pallas_call(finish_kernel, out_shape=(f(1, slots), f(64, 81), f(64, 27...  1.26 us
  transfers between devices with their start and end apart: 7, of which 4 were waited for; matrix products, arithmetic and copies ran while one was open for 1% of the time, Pallas kernels for 15%

commit v1 on v0

--- a/solution.py
+++ b/solution.py
@@ -68,7 +68,13 @@
 
 
 def tile_places():
-    return [(q, w, h, 2 * q + w, 2 * q + h) for q in range(2) for w in range(6) for h in range(2)]
+    return [(q, z, h, 2 * q + h) for q in range(2) for z in range(3 * q, 3 * q + 5) for h in range(2)]
+
+
+def place_row(q, z, k):
+    if 4 * q <= z < 4 * q + 4:
+        return k * 256 + (z - 4 * q) * 64
+    return 2304 + k // 3 * 256 + k % 3 * 64
 
 
 def exact(a, selector):
@@ -92,35 +98,45 @@
     return iota((1, WIDE), 1) >> 6 == iota((SIDE, 1), 0)
 
 
-def windows(ref, q):
-    return jnp.concatenate(
-        [
-            ref[dx * SLAB : dx * SLAB + ROWS, j * 512 + q * 128 : j * 512 + q * 128 + 384]
-            for dx in range(3)
-            for j in range(3)
-        ],
-        axis=1,
-    )
-
-
-def shifted_store(dst_ref, x, val):
+def windows(ref, more, q):
+    own = [
+        ref[dx * SLAB : dx * SLAB + ROWS, j * 512 + q * 256 : j * 512 + (q + 1) * 256]
+        for dx in range(3)
+        for j in range(3)
+    ]
+    return jnp.concatenate(own + [more[q, dx * SLAB : dx * SLAB + ROWS, :] for dx in range(3)], axis=1)
+
+
+def shifted_store(dst_ref, more, x, val):
     zero = jnp.zeros((1, BLK, WIDE), F32)
     lo, hi = (x + 1) * SLAB, (x + 2) * SLAB
     dst_ref[lo:hi, 0:512] = jnp.concatenate([zero, val[:-1]], axis=0).reshape(SLAB, WIDE).astype(BF16)
     dst_ref[lo:hi, 512:1024] = val.reshape(SLAB, WIDE).astype(BF16)
     dst_ref[lo:hi, 1024:1536] = jnp.concatenate([val[1:], zero], axis=0).reshape(SLAB, WIDE).astype(BF16)
-
-
-def clear_ends(ref):
-    ref[0:SLAB, :] = jnp.zeros((SLAB, 1536), BF16)
-    ref[9 * SLAB :, :] = jnp.zeros((SLAB, 1536), BF16)
+    left = iota((SLAB, 128), 1) < 64
+    zero = zero[:, :, :128]
+    for q in range(2):
+        part = val[:, :, 256:384] if q == 0 else val[:, :, 128:256]
+        near = [jnp.concatenate([zero, part[:-1]], axis=0), part, jnp.concatenate([part[1:], zero], axis=0)]
+        near = [v.reshape(SLAB, 128) for v in near]
+        turn = (1,) if q == 0 else (0, 2)
+        near = [pltpu.roll(v, 64, 1) if j in turn else v for j, v in enumerate(near)]
+        more[q, lo:hi, 0:128] = jnp.where(left, near[0], near[1]).astype(BF16)
+        more[q, lo:hi, 128:256] = jnp.where(left, near[2], 0.0).astype(BF16)
+
+
+def clear_ends(ref, more):
+    for at in (0, 9 * SLAB):
+        ref[at : at + SLAB, :] = jnp.zeros((SLAB, 1536), BF16)
+        for q in range(2):
+            more[q, at : at + SLAB, :] = jnp.zeros((SLAB, 256), BF16)
 
 
 def forward_kernel(
     vel_in, tgt_in, w1_in, w2_in, w3_in, own_in, blk_in,
     keep, send, eddy_out, loss_out, dl_out, ah_s, slope1_s, i1_s, dh_s, tb_s, vel, own, blk,
     pool_s, fp_s, a_s, tt_s, pre_s, slope2_s, dw_s, big_s, gh_s, w2_s,
-    tgt, w1, w2, w3, sems,
+    tgt, w1, w2, w3, sems, ea_s,
 ):
     pairs = ((w2_in, w2), (vel_in, vel), (tgt_in, tgt), (w1_in, w1), (w3_in, w3), (own_in, own), (blk_in, blk))
     copies = [pltpu.make_async_copy(src, dst, sems.at[n]) for n, (src, dst) in enumerate(pairs)]
@@ -130,12 +146,16 @@
     trainers = lax.axis_size("gx") * lax.axis_size("gy") * lax.axis_size("role")
 
     fp_s[...] = jnp.zeros(fp_s.shape, F32)
-    clear_ends(a_s)
+    clear_ends(a_s, ea_s)
     w2_s[:, 1664:1792] = jnp.zeros((64, 128), F32)
     zero_tile = jnp.zeros((64, 128), BF16)
-    for q, w, h, z, m in tile_places():
+    for q in range(2):
+        for dx in range(3):
+            for ref in (tt_s, tb_s):
+                ref[q, 2304 + dx * 256 + 192 : 2304 + (dx + 1) * 256, :] = jnp.zeros((64, 256), BF16)
+    for q, z, h, m in tile_places():
         for k in range(9):
-            at, cols = k * 384 + w * 64, slice(h * 128, (h + 1) * 128)
+            at, cols = place_row(q, z, k), slice(h * 128, (h + 1) * 128)
             if not -1 <= z - 2 * m <= 2:
                 tt_s[q, at : at + 64, cols] = zero_tile
                 tb_s[q, at : at + 64, cols] = zero_tile
@@ -167,7 +187,7 @@
     src = iota((256, 1), 0)
     pick = onehot(jnp.where(lane_in < 216, lane_cz, -1) == (src >> 6) * 8 + (src & 7))
     cells = nn(by_block, pick)
-    pick_t = onehot(jnp.where(src >= 192, src & 7, -1) == iota((1, SIDE), 1))
+    pick_t = onehot(jnp.where(src >= 192, src & 7, -1) == iota((1, 24), 1) & 7)
     target = nn(by_block, pick_t)
 
     fp_s[1:9, 1:9] = cells.reshape(SIDE, SIDE, BLK, 256)
@@ -183,15 +203,16 @@
     j_off, j_dz, j_c = lax.div(j_at, 9), lax.rem(lax.div(j_at, 3), 3) - 1, lax.rem(j_at, 3)
     lane_key = jnp.where(lane_in < 216, lane_off * 4 + (lane_cz >> 3), -1)
     same = lane_key == j_off * 4 + j_c
-    delta = jnp.where(same, (lane_in & 7) - j_dz, -9)
     w1v = w1[...]
-    t1 = jnp.concatenate([nn(w1v, onehot(delta == z)).astype(BF16) for z in range(SIDE)], axis=0)
+    by_dz = [nn(w1v, onehot(jnp.where(same, j_dz, 9) == dz)) for dz in (-1, 0, 1)]
+    z_in = jnp.broadcast_to(lane_in & 7, (CH, 256))
+    t1 = []
+    for z in range(SIDE):
+        rows = jnp.where(z_in == z - 1, by_dz[0], jnp.where(z_in == z, by_dz[1], 0.0))
+        t1.append(jnp.where(z_in == z + 1, by_dz[2], rows).astype(BF16))
+    t1 = jnp.concatenate(t1, axis=0)
     pre_s[...] = nt(i1_s[...], t1)
 
-    src = iota((320, 1), 0) - 64
-    dst = iota((1, 512), 1)
-    wanted = ((dst >> 7) - 2 + ((dst & 127) >> 6)) * 64 + (dst & 63)
-    chooser = onehot(jnp.where((src >= 0) & (src < 192), src - 64, -999) == wanted)
     left = iota((64, 128), 1) < 64
     w2_s[:, 0:1728] = w2[...].astype(F32)
     w2t = jnp.concatenate(
@@ -203,30 +224,35 @@
     )
     for k in range(9):
         base = (192 * k) // 128 * 128
-        off = 192 * k - base
-        width = min(256, 1728 - base)
-        tiles = nn(w2[:, base : base + width], chooser[64 - off : 64 - off + width]).astype(BF16)
+        one, two = w2_s[:, base : base + 128], w2_s[:, base + 128 : base + 256]
+        one_r, two_r = pltpu.roll(one, 64, 1), pltpu.roll(two, 64, 1)
+        if k % 2 == 0:
+            low, high = (one, one_r, two), (one_r, one, two_r)
+        else:
+            low, high = (one_r, two, two_r), (one, two_r, two)
+        low, high = (0.0,) + low, high + (0.0,)
+        tiles = {d: jnp.where(left, low[d + 2], high[d + 2]).astype(BF16) for d in (-2, -1, 0, 1)}
         kb = 8 - k
         turned = {dz: w2t[(3 * k + dz + 1) * 64 : (3 * k + dz + 2) * 64] for dz in (-1, 0, 1)}
         turned[-2] = turned[2] = jnp.zeros((64, 128), F32)
         forward = {d: jnp.where(left, turned[d], turned[d - 1]).astype(BF16) for d in (-1, 0, 1, 2)}
-        for q, w, h, z, m in tile_places():
-            at, cols = k * 384 + w * 64, slice(h * 128, (h + 1) * 128)
+        for q, z, h, m in tile_places():
+            at, cols = place_row(q, z, k), slice(h * 128, (h + 1) * 128)
             if z - 2 * m in forward:
                 tt_s[q, at : at + 64, cols] = forward[z - 2 * m]
             d = 2 * m - z
-            at = kb * 384 + w * 64
-            if -2 <= d <= 1:
-                tb_s[q, at : at + 64, cols] = tiles[:, (d + 2) * 128 : (d + 3) * 128]
+            at = place_row(q, z, kb)
+            if d in tiles:
+                tb_s[q, at : at + 64, cols] = tiles[d]
 
     for x in range(SIDE):
         pre = pre_s[x * SLAB : (x + 1) * SLAB, :]
         sig = sigmoid(pre)
         slope1_s[x * SLAB : (x + 1) * SLAB, :] = sig * (1.0 + pre * (1.0 - sig))
-        shifted_store(a_s, x, (pre * sig).reshape(SIDE, BLK, WIDE))
+        shifted_store(a_s, ea_s, x, (pre * sig).reshape(SIDE, BLK, WIDE))
 
     for q in range(2):
-        pre_s[:, q * 256 : (q + 1) * 256] = nn(windows(a_s, q), tt_s[q])
+        pre_s[:, q * 256 : (q + 1) * 256] = nn(windows(a_s, ea_s, q), tt_s[q])
     for x in range(SIDE):
         pre = pre_s[x * SLAB : (x + 1) * SLAB, :]
         sig = sigmoid(pre)
@@ -237,23 +263,29 @@
     w3_wide = nn(w3[...], tile8)
     diag = diagonal()
     last = jnp.where(diag, w3_wide, 0.0).astype(BF16)
-    logits = nt(ah_s[...], last)
+    last3 = jnp.concatenate([jnp.where(diag, w3_wide, 0.0)] * 3, axis=0).astype(BF16)
+    logits = nt(ah_s[...], last3)
     eddy = 0.5 * (jnp.maximum(logits, 0.0) + jnp.log1p(jnp.exp(-jnp.abs(logits))))
     error = eddy - target
-    losses = jnp.sum(jnp.sum((error * error).reshape(64, BLK, SIDE), axis=0), axis=1, keepdims=True) / CELLS
+    lane24 = iota((1, 24), 1)
+    squares = jnp.where(lane24 < SIDE, error * error, 0.0)
+    losses = jnp.sum(jnp.sum(squares.reshape(64, BLK, 24), axis=0), axis=1, keepdims=True) / CELLS
     d_logit = (error * sigmoid(logits) / (trainers * CELLS)).astype(BF16)
 
-    zrep = onehot(iota((SIDE, 1), 0) == (iota((1, 128), 1) & 15) >> 1)
-    fine = exact(eddy, zrep)
+    zrep = onehot(iota((24, 1), 0) & 7 == (iota((1, 128), 1) & 15) >> 1)
+    e_high = eddy.astype(BF16).astype(F32)
+    e_mid = (eddy - e_high).astype(BF16).astype(F32)
+    e_parts = jnp.where(lane24 < 8, e_high, jnp.where(lane24 < 16, e_mid, eddy - e_high - e_mid))
+    fine = nn(e_parts.astype(BF16), zrep)
     fine = jnp.where(iota((1, 128), 1) >> 4 == iota((ROWS, 1), 0) & 7, fine, 0.0)
     fine = jnp.sum(fine.reshape(64, BLK, 128), axis=1)
     eddy_out[...] = fine
     y_face(send.at[HIDDEN_TILES * 32 : HIDDEN_TILES * 32 + 104], vel, eddy_out, gy_at & 1 == 0)
     loss_out[...] = jnp.broadcast_to(losses, (BLK, 128))
-    dl_out[...] = d_logit.astype(F32)
+    dl_out[...] = d_logit.astype(F32)[:, 0:SIDE]
 
     count = times_sampled(own, blk, gx_at)
-    big_s[:, 0:512] = nn(d_logit, last)
+    big_s[:, 0:512] = nn(d_logit, jnp.concatenate([last.astype(F32), jnp.zeros((16, WIDE), F32)], axis=0).astype(BF16))
     for x in range(SIDE):
         d_hid = big_s[x * SLAB : (x + 1) * SLAB, 0:512] * slope2_s[x * SLAB : (x + 1) * SLAB, :]
         d_hid = d_hid.astype(BF16)
@@ -295,17 +327,17 @@
 
 def backward_kernel(
     vel, own, blk, eddy, losses, dl_in, ah_s, slope1_s, i1_s, dh_s, tb_s,
-    extra_out, halo1, halo2, halo3, halo4, hx_a, hx_b, hy_b, hz, d_s, pre_s, dw_s,
+    extra_out, halo1, halo2, halo3, halo4, hx_a, hx_b, hy_b, hz, d_s, pre_s, dw_s, ed_s,
 ):
     gx_at, gy_at, second = place()
     gx_odd, gy_odd = gx_at & 1 == 1, gy_at & 1 == 1
     dev = (gx_at * lax.axis_size("gy") + gy_at) * lax.axis_size("role") + lax.axis_index("role")
     count = times_sampled(own, blk, gx_at)
 
-    clear_ends(d_s)
+    clear_ends(d_s, ed_s)
     for x in range(SIDE):
         d_hid = dh_s[x * SLAB : (x + 1) * SLAB, :].astype(F32)
-        shifted_store(d_s, x, d_hid.reshape(SIDE, BLK, WIDE))
+        shifted_store(d_s, ed_s, x, d_hid.reshape(SIDE, BLK, WIDE))
 
     for c in range(3):
         for i in range(2):
@@ -332,7 +364,7 @@
     halo4[...] = jnp.where(second, hz[...], hx_b[...])
 
     for q in range(2):
-        pre_s[:, q * 256 : (q + 1) * 256] = nn(windows(d_s, q), tb_s[q])
+        pre_s[:, q * 256 : (q + 1) * 256] = nn(windows(d_s, ed_s, q), tb_s[q])
     for x in range(SIDE):
         rows = slice(x * SLAB, (x + 1) * SLAB)
         d_first = (pre_s[rows, :] * slope1_s[rows, :]).astype(BF16).astype(F32)
@@ -361,8 +393,10 @@
     ah = ah_s[...]
     gl = tn(dl_hi, ah) + tn(dl_lo, ah)
     gl = jnp.where(diagonal(), gl, 0.0)
-    fold_o = onehot(iota((1, WIDE), 1) & 63 == iota((64, 1), 0), F32)
-    g_last = jnp.sum(nt(fold_o, gl, HIGH), axis=1, keepdims=True)
+    gl = jnp.sum(gl, axis=0, keepdims=True)
+    gl = gl[:, 0:128] + gl[:, 128:256] + gl[:, 256:384] + gl[:, 384:512]
+    at_lane = iota((1, 128), 1) & 63 == iota((64, 1), 0)
+    g_last = jnp.sum(jnp.where(at_lane, gl, 0.0), axis=1, keepdims=True)
 
     lane8 = iota((BLK, 128), 1)
     loss_row = jnp.where(lane8 - (LOSS_COL + BLK * (dev >> 6)) == iota((BLK, 128), 0), losses[...], 0.0)
@@ -393,7 +427,7 @@
             pltpu.VMEM((ROWS, WIDE), F32),
             pltpu.VMEM((ROWS, 256), BF16),
             pltpu.VMEM((ROWS, WIDE), BF16),
-            pltpu.VMEM((2, 3456, 256), BF16),
+            pltpu.VMEM((2, 3072, 256), BF16),
         )
         + tuple(pltpu.VMEM(a.shape, a.dtype) for a in (velocity, own, blk)),
         in_specs=[pl.BlockSpec(memory_space=pltpu.HBM)] * 7,
@@ -402,7 +436,7 @@
             pltpu.VMEM((3, SIDE, 16, 128), F32),
             pltpu.VMEM((10, 10, BLK, 256), F32),
             pltpu.VMEM((ROWS + 2 * SLAB, 1536), BF16),
-            pltpu.VMEM((2, 3456, 256), BF16),
+            pltpu.VMEM((2, 3072, 256), BF16),
             pltpu.VMEM((ROWS, WIDE), F32),
             pltpu.VMEM((ROWS, WIDE), F32),
             pltpu.VMEM((ROWS, WIDE), BF16),
@@ -411,7 +445,7 @@
             pltpu.VMEM((64, 1792), F32),
         ]
         + [pltpu.VMEM(a.shape, a.dtype) for a in (target, w1, w2, w3)]
-        + [pltpu.SemaphoreType.DMA((7,))],
+        + [pltpu.SemaphoreType.DMA((7,)), pltpu.VMEM((2, ROWS + 2 * SLAB, 256), BF16)],
         compiler_params=pltpu.CompilerParams(vmem_limit_bytes=40 * 1024 * 1024),
         name="forward",
     )(velocity, target, w1, w2, w3, own, blk)
@@ -429,6 +463,7 @@
             pltpu.VMEM((ROWS + 2 * SLAB, 1536), BF16),
             pltpu.VMEM((ROWS, WIDE), F32),
             pltpu.VMEM((ROWS, WIDE), BF16),
+            pltpu.VMEM((2, ROWS + 2 * SLAB, 256), BF16),
         ],
         compiler_params=pltpu.CompilerParams(vmem_limit_bytes=40 * 1024 * 1024),
         name="backward",

time: 39.8 us -> 39.2 us (0.985)
  Pallas kernels: 14.6 us -> 14 us
    pallas_call x1, Pallas kernels: 3.42 us -> 2.89 us  [run_backward(): pl.pallas_call(backward_kernel, out_shape=(pltpu.VMEM((64, 128), F32),) +...]
  transfers between devices with their start and end apart: 7 -> 7, of which waited for: 4 -> 4; matrix products, arithmetic and copies ran while one was open for 1% -> 1% of each run, Pallas kernels for 15% -> 14%
where the time goes in v1:
time: 39.2 us; the launch traced here: 39 us
  Pallas kernels  14 us (36%)
  starting transfers between devices  12.6 us (32%)
  waiting for transfers between devices  10.8 us (28%)
  between operations  0.82 us (2%)
  other arithmetic  0.76 us (2%)
    ppermute x4, waiting for transfers between devices, on_device(): got = lax.ppermute(message, axes, mixed(kinds))  9.31 us
    ppermute x4, starting transfers between devices, on_device(): got = lax.ppermute(message, axes, mixed(kinds))  8.4 us
    pallas_call x1, Pallas kernels, run_forward(): pl.pallas_call(forward_kernel, out_shape=(half, pltpu.VMEM((HIDDEN_TILES...  7.19 us
    ppermute x1, starting transfers between devices, on_device(): far = lax.ppermute(halos[3], axes, mixed((orders[0][3], orders[1][3])))  3.67 us
    pallas_call x1, Pallas kernels, run_backward(): pl.pallas_call(backward_kernel, out_shape=(pltpu.VMEM((64, 128), F32),) +...  2.89 us
    pallas_call x1, Pallas kernels, run_flow(): pl.pallas_call(flow_kernel, out_shape=jax.ShapeDtypeStruct(velocity.shape...  2.62 us
    ppermute x1, waiting for transfers between devices, on_device(): other = lax.ppermute(total, 'gy', core_pairs)  1.52 us
    pallas_call x1, Pallas kernels, run_finish(): pl.pallas_call(finish_kernel, out_shape=(f(1, slots), f(64, 81), f(64, 27...  1.25 us
  transfers between devices with their start and end apart: 7, of which 4 were waited for; matrix products, arithmetic and copies ran while one was open for 1% of the time, Pallas kernels for 14%

profile of v1, /device:TPU:0, one launch (start us, length us, event | category | flops | bytes accessed | tf_op | source)
XLA Modules:
  0.0 39.0 jit_solution(9758870450777854925)
XLA Ops:
  0.6 7.2 %forward.1 = (f32[448,128]{1,0:T(8,128)S(1)}, f32[552,128]{1,0:T(8,128)S(1)}, f32[64,128]{1,0:T(8,128)S(1)}, f32[8,128]{1,0:T(8,128)S(1)}, f32[512,8]{1,0:T(8,12...) custom-call(f32[3,16,16,128]{3,2,1,0:T(8,128)} %vel_in.1, ...), custom_call_target="tpu_custom_call" | custom-call | tf_op jit(solution)/shard_map/forward/pallas_call | solution.py:418
  7.8 0.5 %collective-permute-start = (f32[552,128]{1,0:T(8,128)S(1)}, f32[552,128]{1,0:T(8,128)S(1)}, u32[]{:S(2)}, u32[]{:S(2)}) collective-permute-start(f32[552,128]{1,0:T(8,128)S(1)} %get-tuple-element.32), channel_id=1, source_target_pairs={{0,2},{2,0},{4,6},{6,4},{1,3},{3,1},{5,7},{7,5},{8,10},{10,8},{12,... | collective-permute-start | bytes 847880 | tf_op jit(solution)/shard_map/ppermute | solution.py:676
  8.3 2.9 %backward.1 = (f32[64,128]{1,0:T(8,128)S(1)}, f32[104,128]{1,0:T(8,128)S(1)}, f32[104,128]{1,0:T(8,128)S(1)}, f32[104,128]{1,0:T(8,128)S(1)}, f32[104,128]{1,0:T(8,128)S(1)}) custom-call(f32[3,16,16,128]{3,2,1,0:T(8,128)S(1)} %get-tuple-element.33.vel, s32[1,32]{1,0:T(1,128)S(1)} %get-tuple-element.34.own, s32[1,32]{1,0:T(1,128)S(1)} %get-tuple-element.35.blk, ...), custom_call_target="tpu_custom_call" | custom-call | tf_op jit(solution)/shard_map/backward/pallas_call | solution.py:456
  11.3 0.0 collective-permute-done
  11.4 0.1 pad_maximum_fusion.1
  11.5 2.7 %collective-permute-start.1 = (f16[632,128]{1,0:T(8,128)(2,1)S(1)}, f16[632,128]{1,0:T(8,128)(2,1)S(1)}, u32[]{:S(2)}, u32[]{:S(2)}) collective-permute-start(f16[632,128]{1,0:T(8,128)(2,1)S(1)} %pad_maximum_fusion.1), channel_id=1, source_target_pairs={{0,6},{1,7},{2,10},{3,11},{4,12},{5,13},{6,0},{7,1},{8,14},{9,15},... | collective-permute-start | bytes 485384 | tf_op jit(solution)/shard_map/ppermute | solution.py:695
  14.2 3.7 %collective-permute-start.3 = (f16[104,128]{1,0:T(8,128)(2,1)S(1)}, f16[104,128]{1,0:T(8,128)(2,1)S(1)}, u32[]{:S(2)}, u32[]{:S(2)}) collective-permute-start(f16[104,128]{1,0:T(8,128)(2,1)S(1)} %convert_element_type.96), channel_id=1, source_target_pairs={{0,24},{1,25},{2,3},{3,2},{4,5},{5,4},{6,30},{7,31},{8,16},{9,17},... | collective-permute-start | bytes 79880 | tf_op jit(solution)/shard_map/ppermute | solution.py:697
  17.9 0.0 collective-permute-done.1
  17.9 0.1 fusion.5
  18.0 0.1 pad_maximum_fusion.2
  18.0 1.1 %collective-permute-start.2 = (f16[632,128]{1,0:T(8,128)(2,1)S(1)}, f16[632,128]{1,0:T(8,128)(2,1)S(1)}, u32[]{:S(2)}, u32[]{:S(2)}) collective-permute-start(f16[632,128]{1,0:T(8,128)(2,1)S(1)} %pad_maximum_fusion.2), channel_id=1, source_target_pairs={{0,8},{1,9},{2,4},{3,5},{4,2},{5,3},{6,14},{7,15},{8,0},{9,1},{10,... | collective-permute-start | bytes 485384 | tf_op jit(solution)/shard_map/ppermute | solution.py:695
  19.1 4.3 %collective-permute-done.2 = f16[632,128]{1,0:T(8,128)(2,1)S(1)} collective-permute-done((f16[632,128]{1,0:T(8,128)(2,1)S(1)}, f16[632,128]{1,0:T(8,128)(2,1)S(1)}, u32[]{:S(2)}, u32[]{:S(2)}) %collective-permute-start.2) | collective-permute-done | bytes 161824 | tf_op jit(solution)/shard_map/ppermute | solution.py:695
  23.4 0.1 fusion.4
  23.6 0.1 pad_maximum_fusion.3
  23.6 1.6 %collective-permute-start.4 = (f16[632,128]{1,0:T(8,128)(2,1)S(1)}, f16[632,128]{1,0:T(8,128)(2,1)S(1)}, u32[]{:S(2)}, u32[]{:S(2)}) collective-permute-start(f16[632,128]{1,0:T(8,128)(2,1)S(1)} %pad_maximum_fusion.3), channel_id=1, source_target_pairs={{0,1},{1,0},{2,26},{3,27},{4,28},{5,29},{6,7},{7,6},{8,9},{9,8},{1... | collective-permute-start | bytes 485384 | tf_op jit(solution)/shard_map/ppermute | solution.py:695
  25.2 3.8 %collective-permute-done.4 = f16[632,128]{1,0:T(8,128)(2,1)S(1)} collective-permute-done((f16[632,128]{1,0:T(8,128)(2,1)S(1)}, f16[632,128]{1,0:T(8,128)(2,1)S(1)}, u32[]{:S(2)}, u32[]{:S(2)}) %collective-permute-start.4) | collective-permute-done | bytes 161824 | tf_op jit(solution)/shard_map/ppermute | solution.py:695
  29.0 0.1 fusion.1
  29.1 3.1 %collective-permute-start.5 = (f16[528,128]{1,0:T(8,128)(2,1)S(1)}, f16[528,128]{1,0:T(8,128)(2,1)S(1)}, u32[]{:S(2)}, u32[]{:S(2)}) collective-permute-start(f16[528,128]{1,0:T(8,128)(2,1)S(1)} %pad_maximum_fusion.4), channel_id=1, source_target_pairs={{0,24},{1,25},{2,3},{3,2},{4,5},{5,4},{6,30},{7,31},{8,16},{9,17},... | collective-permute-start | bytes 405512 | tf_op jit(solution)/shard_map/ppermute | solution.py:695
  32.2 2.6 %flow.1 = f32[3,16,16,128]{3,2,1,0:T(8,128)} custom-call(f32[3,16,16,128]{3,2,1,0:T(8,128)S(1)} %get-tuple-element.33.vel, f32[64,128]{1,0:T(8,128)S(1)} %get-tuple-element.36.eddy, f32[104,128]{1,0:T(8,128)S(1)} %slice.81.got0, f32[104,128]{1,0:T(8,128)S(1)} %slice_convert_fusion.2.got1, f32[104,128]{1,0:T(8,128)S(1)} %slice_convert_fusion.1.got2, ...), custom_call_target="tpu_custom_call" | custom-call | tf_op jit(solution)/shard_map/flow/pallas_call | solution.py:574
  34.9 1.2 %collective-permute-done.5 = f16[528,128]{1,0:T(8,128)(2,1)S(1)} collective-permute-done((f16[528,128]{1,0:T(8,128)(2,1)S(1)}, f16[528,128]{1,0:T(8,128)(2,1)S(1)}, u32[]{:S(2)}, u32[]{:S(2)}) %collective-permute-start.5) | collective-permute-done | bytes 135200 | tf_op jit(solution)/shard_map/ppermute | solution.py:695
  36.1 0.1 fusion.mine
  36.2 0.1 collective-permute-start.6
  36.2 1.5 %collective-permute-done.6.other = f32[512,128]{1,0:T(8,128)S(1)} collective-permute-done((f32[512,128]{1,0:T(8,128)S(1)}, f32[512,128]{1,0:T(8,128)S(1)}, u32[]{:S(2)}, u32[]{:S(2)}) %collective-permute-start.6) | collective-permute-done | bytes 262176 | tf_op jit(solution)/shard_map/ppermute | solution.py:714
  37.8 1.3 %finish.1 = (f32[1,8]{1,0:T(1,128)}, f32[64,81]{1,0:T(8,128)}, f32[64,1728]{1,0:T(8,128)}, f32[1,64]{1,0:T(1,128)}) custom-call(s32[1,32]{1,0:T(1,128)S(1)} %get-tuple-element.34.own, s32[1,32]{1,0:T(1,128)S(1)} %get-tuple-element.35.blk, f32[512,128]{1,0:T(8,128)S(1)} %fusion.mine, f32[512,128]{1,0:T(8,128)S(1)} %collective-permute-done.6.other), custom_call_target="tpu_custom_call" | custom-call | tf_op jit(solution)/shard_map/finish/pallas_call | solution.py:625
  (21 shorter events, 0.3 us)
Async XLA Ops:
  7.8 3.4 %collective-permute-start = (f32[552,128]{1,0:T(8,128)S(1)}, f32[552,128]{1,0:T(8,128)S(1)}, u32[]{:S(2)}, u32[]{:S(2)}) collective-permute-start(f32[552,128]{1,0:T(8,128)S(1)} %get-tuple-element.32), channel_id=1, source_target_pairs={{0,2},{2,0},{4,6},{6,4},{1,3},{3,1},{5,7},{7,5},{8,10},{10,8},{12,... | collective-permute-start | bytes 847880 | tf_op jit(solution)/shard_map/ppermute | solution.py:676
  11.5 6.4 %collective-permute-start.1 = (f16[632,128]{1,0:T(8,128)(2,1)S(1)}, f16[632,128]{1,0:T(8,128)(2,1)S(1)}, u32[]{:S(2)}, u32[]{:S(2)}) collective-permute-start(f16[632,128]{1,0:T(8,128)(2,1)S(1)} %pad_maximum_fusion.1), channel_id=1, source_target_pairs={{0,6},{1,7},{2,10},{3,11},{4,12},{5,13},{6,0},{7,1},{8,14},{9,15},... | collective-permute-start | bytes 485384 | tf_op jit(solution)/shard_map/ppermute | solution.py:695
  14.2 9.3 %collective-permute-start.3 = (f16[104,128]{1,0:T(8,128)(2,1)S(1)}, f16[104,128]{1,0:T(8,128)(2,1)S(1)}, u32[]{:S(2)}, u32[]{:S(2)}) collective-permute-start(f16[104,128]{1,0:T(8,128)(2,1)S(1)} %convert_element_type.96), channel_id=1, source_target_pairs={{0,24},{1,25},{2,3},{3,2},{4,5},{5,4},{6,30},{7,31},{8,16},{9,17},... | collective-permute-start | bytes 79880 | tf_op jit(solution)/shard_map/ppermute | solution.py:697
  18.0 5.4 %collective-permute-start.2 = (f16[632,128]{1,0:T(8,128)(2,1)S(1)}, f16[632,128]{1,0:T(8,128)(2,1)S(1)}, u32[]{:S(2)}, u32[]{:S(2)}) collective-permute-start(f16[632,128]{1,0:T(8,128)(2,1)S(1)} %pad_maximum_fusion.2), channel_id=1, source_target_pairs={{0,8},{1,9},{2,4},{3,5},{4,2},{5,3},{6,14},{7,15},{8,0},{9,1},{10,... | collective-permute-start | bytes 485384 | tf_op jit(solution)/shard_map/ppermute | solution.py:695
  23.6 5.4 %collective-permute-start.4 = (f16[632,128]{1,0:T(8,128)(2,1)S(1)}, f16[632,128]{1,0:T(8,128)(2,1)S(1)}, u32[]{:S(2)}, u32[]{:S(2)}) collective-permute-start(f16[632,128]{1,0:T(8,128)(2,1)S(1)} %pad_maximum_fusion.3), channel_id=1, source_target_pairs={{0,1},{1,0},{2,26},{3,27},{4,28},{5,29},{6,7},{7,6},{8,9},{9,8},{1... | collective-permute-start | bytes 485384 | tf_op jit(solution)/shard_map/ppermute | solution.py:695
  29.1 7.0 %collective-permute-start.5 = (f16[528,128]{1,0:T(8,128)(2,1)S(1)}, f16[528,128]{1,0:T(8,128)(2,1)S(1)}, u32[]{:S(2)}, u32[]{:S(2)}) collective-permute-start(f16[528,128]{1,0:T(8,128)(2,1)S(1)} %pad_maximum_fusion.4), channel_id=1, source_target_pairs={{0,24},{1,25},{2,3},{3,2},{4,5},{5,4},{6,30},{7,31},{8,16},{9,17},... | collective-permute-start | bytes 405512 | tf_op jit(solution)/shard_map/ppermute | solution.py:695
  36.2 1.6 %collective-permute-start.6 = (f32[512,128]{1,0:T(8,128)S(1)}, f32[512,128]{1,0:T(8,128)S(1)}, u32[]{:S(2)}, u32[]{:S(2)}) collective-permute-start(f32[512,128]{1,0:T(8,128)S(1)} %fusion.mine), channel_id=1, source_target_pairs={{0,2},{2,0},{4,6},{6,4},{1,3},{3,1},{5,7},{7,5},{8,10},{10,8},{12,... | collective-permute-start | bytes 786440 | tf_op jit(solution)/shard_map/ppermute | solution.py:714
